TPU v7x, 32 devices: a whole 2x2x4 slice. The times are simulated.
32 devices in a mesh: group: 16 (over z, y, core), inner: 2 (over x).
Axes of the slice: x: 2, y: 2, z: 4, core: 2. Of those that a mesh axis runs over, the one named last changes fastest.
Arguments:
- tokens: bfloat16 [16384, 768], P(('group', 'inner')), may hold values from -6 to 6
- cotangent: bfloat16 [16384, 768], P(('group', 'inner')), may hold values from -6 to 6
- segments: int32 [32, 512], P(('group', 'inner')), may hold values from 0 to 7, never falling along the last dimension, each value on 1 to 256 neighbouring positions
- w_qkv: bfloat16 [3, 768, 768], P(None, 'group', 'inner'), may hold values from -0.21875 to 0.21875
- w_out: bfloat16 [768, 768], P('group', 'inner'), may hold values from -1.75 to 1.75
- w_up: bfloat16 [768, 3072], P('group', 'inner'), may hold values from -0.21875 to 0.21875
- w_down: bfloat16 [3072, 768], P('inner', 'group'), may hold values from -0.109375 to 0.109375
- rel_embed: bfloat16 [512, 768], P('group', 'inner'), may hold values from -6 to 6
- attn_bias: bfloat16 [4, 768], replicated, may hold values from -3 to 3
- up_bias: bfloat16 [3072], replicated, may hold values from -3 to 3
- down_bias: bfloat16 [768], replicated, may hold values from -3 to 3
- norm_gain: bfloat16 [2, 768], replicated, may hold values from 0.5 to 1.5
- norm_bias: bfloat16 [2, 768], replicated, may hold values from -3 to 3
- attn_p: float32 [768, 4, 12], replicated, may hold values from -1.75 to 1.75
- attn_q: float32 [768, 4, 12], replicated, may hold values from -0.21875 to 0.21875
- up_p: float32 [3072, 12], replicated, may hold values from -1.75 to 1.75
- up_q: float32 [768, 12], replicated, may hold values from -0.21875 to 0.21875
- down_p: float32 [768, 12], replicated, may hold values from -1.75 to 1.75
- down_q: float32 [3072, 12], replicated, may hold values from -0.109375 to 0.109375
- lam: float32 [6, 12], replicated, may hold values from -3 to 3
Outputs:
- layer_out: bfloat16 [16384, 768], P(('group', 'inner'))
- grad_tokens: bfloat16 [16384, 768], P(('group', 'inner'))
- grad_attn_p: float32 [768, 4, 12], P('inner')
- grad_attn_q: float32 [768, 4, 12], P('inner')
- grad_up_p: float32 [3072, 12], P('inner')
- grad_up_q: float32 [768, 12], P('inner')
- grad_down_p: float32 [768, 12], P('inner')
- grad_down_q: float32 [3072, 12], P('inner')
- grad_lam: float32 [6, 12], replicated
Inputs may be any that keep to these rules, and one draw needn't show every extreme that they name: `segments`: within each packed row segment numbers never fall, every document has at most 256 tokens and some document has exactly that many.
All inputs are finite; a program needn't handle non-finite values.
Results may differ from a plain program's by a relative error of at most 0.02.
The roundings to bfloat16 on the way count: a program that leaves them out, or rounds other values in their place, can miss the bound.
Values may be sent and summed in bfloat16 or wider, within the bound.
A program may use at most 256 MiB of HBM per device.

v0:
```python
import functools

import jax
import jax.numpy as jnp
import numpy as np
from jax import lax
from jax.experimental import pallas as pl
from jax.experimental.pallas import tpu as pltpu
from jax.sharding import PartitionSpec as P

D = 768
H = 12
DH = 64
FF = 3072
SPAN = 256
L = 512
R = 12
HALF = L // 2
SCALE = (3.0 * DH) ** (-0.5)
EPS = 1e-07

bf16 = jnp.bfloat16
f32 = jnp.float32


def bucket_values(offsets, span_size):
    middle = span_size // 2
    magnitude = np.abs(offsets)
    inside = magnitude <= middle
    clipped = np.maximum(magnitude, middle) * 1.0
    logged = (
        np.ceil(np.log(clipped / middle) / np.log((2 * span_size - 1) / middle) * (middle - 1))
        + middle
    )
    bucket = np.where(inside, offsets, np.sign(offsets) * logged.astype(np.int32))
    return np.clip(bucket + span_size, 0, 2 * span_size - 1).astype(np.int32)


def bucket_rows():
    offsets = np.minimum(np.arange(2 * HALF) - (HALF - 1), HALF - 1)
    far = bucket_values(offsets, SPAN)
    near = bucket_values(-offsets, SPAN)
    return np.stack([near, far]).astype(np.int32)


def mm(a, b):
    return lax.dot_general(a, b, (((1,), (0,)), ((), ())), preferred_element_type=f32)


def mm_t(a, b):
    return lax.dot_general(a, b, (((1,), (1,)), ((), ())), preferred_element_type=f32)


def tmm(a, b):
    return lax.dot_general(a, b, (((0,), (0,)), ((), ())), preferred_element_type=f32)


def iota(shape, dim):
    return lax.broadcasted_iota(jnp.int32, shape, dim)


def loop(count, body):
    def step(index, carry):
        body(index)
        return carry

    lax.fori_loop(0, count, step, 0)


def block(index, size):
    return pl.ds(pl.multiple_of(index * size, size), size)


def mean_row(values):
    return jnp.sum(values, axis=1, keepdims=True) * (1.0 / D)


def whole(ref):
    return ref[...].reshape(-1, ref.shape[-1])


def columns(ref, cols):
    picked = ref[:, :, :, :, cols]
    return picked.reshape(-1, picked.shape[-1])


SCRATCH = dict(
    shift=((L, L), bf16),
    unshift=((L, L), bf16),
    flip=((HALF, HALF), bf16),
    mask=((2, HALF, HALF), f32),
    tok=((L, D), bf16),
    cot=((L, D), bf16),
    pk_near_t=((D, L), bf16),
    pk_far_t=((D, L), bf16),
    pq_far_t=((D, L), bf16),
    emb_near=((L, D), bf16),
    emb_far=((L, D), bf16),
    q=((L, D), bf16),
    k=((L, D), bf16),
    v=((L, D), bf16),
    qt=((D, L), bf16),
    kt=((D, L), bf16),
    k_rev_t=((D, L), bf16),
    g_t=((D, L), bf16),
    v_rev=((L, D), bf16),
    v_rev_t=((D, L), bf16),
    probs=((H, L, HALF), bf16),
    probs_t=((H, L, HALF), bf16),
    ctx=((L, D), bf16),
    attn_pt=((4 * R, D), bf16),
    attn_qt=((4 * R, D), bf16),
    up_pt=((R, FF), bf16),
    up_qt=((R, D), bf16),
    down_pt=((R, D), bf16),
    down_qt=((R, FF), bf16),
    lam_row=((8, 4 * R), f32),
    lam_col=((4 * R, 1), f32),
    u_t=((4 * R, L), f32),
    du_t=((4 * R, L), bf16),
    u_pos_t=((4 * R, L), f32),
    u_up_t=((R, L), f32),
    u_down_t=((R, L), f32),
    xhat1=((L, D), f32),
    rs1=((L, 1), f32),
    hidden=((L, D), f32),
    hid=((L, D), bf16),
    act=((L, FF), bf16),
    slope=((L, FF), bf16),
    branch=((L, D), f32),
    gsum2=((L, D), f32),
    gb5=((L, D), bf16),
    gpk_t=((D, L), bf16),
    gpq_t=((D, L), bf16),
)

GATHERED = dict(
    wqkv=((3, 4, 2, 2, 48, D), bf16),
    wout=((4, 2, 2, 48, D), bf16),
    wup=((4, 2, 2, 48, FF), bf16),
    wdown=((4, 2, 2, 48, FF), bf16),
    embed=((4, 2, 2, 32, D), bf16),
)

ALIASES = dict(
    gpre="slope",
    gsum1="gsum2",
    gb3="gb5",
    gctx="q",
    gq_t="kt",
    gk_t="pk_near_t",
    gv_t="v_rev_t",
    low_out="layer_out",
)

INPUTS = [
    "tokens",
    "cotangent",
    "segments",
    "buckets",
    "attn_bias",
    "up_bias",
    "down_bias",
    "norm_gain",
    "norm_bias",
    "attn_p",
    "attn_q",
    "up_p",
    "up_q",
    "down_p",
    "down_q",
    "lam",
]
SHARDS = [name + "_shard" for name in GATHERED]
IN_HBM = ["tokens", "cotangent"]
OUTPUTS = ["layer_out", "grad_tokens"]
GRADS = dict(
    grad_wide=((2 * R, FF), f32),
    grad_narrow=((2 * R, D), f32),
    grad_fourth=((2 * R, D), f32),
    grad_attn=((6 * R, D), f32),
    grad_lam=((8, 128), f32),
)


class Refs:
    pass


def as_column(row):
    return jnp.transpose(jnp.broadcast_to(row, (128, row.shape[1])))[:, 0:1]


def rank_group(n):
    rank = iota((4 * R, 1), 0)
    return ((rank >= R * n) & (rank < R * (n + 1))).astype(f32)


def prepare_masks(r):
    seg_row = r.segments[...]
    seg_col = as_column(seg_row)
    same = (seg_col == seg_row).astype(f32)
    width = jnp.sum(same, axis=0, keepdims=True)
    place = iota((1, L), 1).astype(f32)
    start = jnp.min(jnp.where(width == float(HALF), place, float(L)), axis=1, keepdims=True)
    row, col = iota((L, L), 0).astype(f32), iota((L, L), 1).astype(f32)
    ahead = row + start
    ahead = jnp.where(ahead >= float(L), ahead - float(L), ahead)
    r.shift[...] = (col == ahead).astype(bf16)
    back = col + start
    back = jnp.where(back >= float(L), back - float(L), back)
    r.unshift[...] = (row == back).astype(bf16)
    r.flip[...] = (iota((HALF, HALF), 0) + iota((HALF, HALF), 1) == HALF - 1).astype(bf16)
    seg_low = jnp.broadcast_to(seg_row.astype(f32), (8, L)).astype(bf16)
    moved_row = mm_t(seg_low, r.shift[...])[0:1, :]
    moved_col = as_column(moved_row)
    for b in range(2):
        rows = slice(HALF * b, HALF * (b + 1))
        r.mask[b] = jnp.where(moved_col[rows, :] == moved_row[:, rows], 0.0, -1e30)


def prepare_factors(r):
    copies = [
        pltpu.make_async_copy(source, target, r.load_sem.at[i])
        for i, (source, target) in enumerate(((r.tokens, r.tok), (r.cotangent, r.cot)))
    ]
    for copy in copies:
        copy.start()
    r.attn_pt[...] = jnp.concatenate([r.attn_p[:, n, :] for n in range(4)], axis=0).astype(bf16)
    r.attn_qt[...] = jnp.concatenate([r.attn_q[:, n, :] for n in range(4)], axis=0).astype(bf16)
    r.up_pt[...] = r.up_p[...].astype(bf16)
    r.up_qt[...] = r.up_q[...].astype(bf16)
    r.down_pt[...] = r.down_p[...].astype(bf16)
    r.down_qt[...] = r.down_q[...].astype(bf16)
    for n in range(4):
        r.lam_row[0:1, R * n : R * (n + 1)] = r.lam[n : n + 1, :]
    r.lam_col[...] = as_column(r.lam_row[0:1, :])
    copies[0].wait()
    r.tok[...] = mm(r.shift[...], r.tok[...]).astype(bf16)
    copies[1].wait()
    r.cot[...] = mm(r.shift[...], r.cot[...]).astype(bf16)


def embed_positions(r):
    column = iota((L, L), 1)
    near_table, far_table = ((as_column(r.buckets[i : i + 1, :]) == column).astype(bf16) for i in range(2))
    r.emb_near[...] = mm(near_table, whole(r.embed)).astype(bf16)
    r.emb_far[...] = mm(far_table, whole(r.embed)).astype(bf16)
    r.u_pos_t[...] = mm_t(r.attn_qt[...], r.emb_far[...])


def project_position(n, near, out, r):
    emb = r.emb_near if near else r.emb_far
    u = mm_t(r.attn_qt[...], emb[...]) if near else r.u_pos_t[...]
    mixed_t = (u * r.lam_col[...] * rank_group(n)).astype(bf16)
    result = (
        mm(emb[...], whole(r.wqkv.at[n]))
        + r.attn_bias[n : n + 1, :].astype(f32)
        + tmm(mixed_t, r.attn_pt[...])
    ).astype(bf16)
    getattr(r, out)[...] = jnp.transpose(result)


def reduce_tokens(r):
    r.u_t[...] = mm_t(r.attn_qt[...], r.tok[...])


def project_token(n, out, r):
    mixed_t = (r.u_t[...] * r.lam_col[...] * rank_group(n)).astype(bf16)
    getattr(r, out)[...] = (
        mm(r.tok[...], whole(r.wqkv.at[n]))
        + r.attn_bias[n : n + 1, :].astype(f32)
        + tmm(mixed_t, r.attn_pt[...])
    ).astype(bf16)


def flip_columns(r, source, target):
    for b in range(2):
        cols = slice(HALF * b, HALF * (b + 1))
        target[:, cols] = mm(source[:, cols], r.flip[...]).astype(bf16)


def arrange_heads(r):
    for b in range(2):
        rows = slice(HALF * b, HALF * (b + 1))
        r.v_rev[rows, :] = mm(r.flip[...], r.v[rows, :]).astype(bf16)
    r.v_rev_t[...] = jnp.transpose(r.v_rev[...])
    r.qt[...] = jnp.transpose(r.q[...])
    r.kt[...] = jnp.transpose(r.k[...])
    flip_columns(r, r.kt, r.k_rev_t)


def head_lanes(a):
    lane = iota((1, 2 * DH), 1)
    return ((lane >= DH) if a else (lane < DH)).astype(bf16)


def attend(r, before=None):
    def pair(p):
        cols = block(p, 2 * DH)
        high = iota((HALF, HALF), 1) + iota((HALF, HALF), 0) >= HALF - 1
        for b in range(2):
            if before is not None:
                before(p, b)
            rows = slice(HALF * b, HALF * (b + 1))
            q, k, v = r.q[rows, cols], r.k[rows, cols], r.v[rows, cols]
            keys = r.kt[cols, rows]
            near_keys, far_queries = r.pk_near_t[cols, :], r.pq_far_t[cols, :]
            probs = []
            for a in range(2):
                lanes = head_lanes(a)
                qa, ka = q * lanes, k * lanes
                content, to, fro = mm(qa, keys), mm(qa, near_keys), mm(ka, far_queries)
                near = jnp.where(high, to[:, :HALF], to[:, HALF:])
                near = pltpu.roll(near, 1, 1, stride=1, stride_axis=0)
                far = jnp.where(high, fro[:, :HALF], fro[:, HALF:])
                far = pltpu.roll(far, 1, 1, stride=1, stride_axis=0)
                scores = (content + near + jnp.transpose(far)) * SCALE + r.mask[b]
                peak = jnp.max(scores, axis=1, keepdims=True)
                terms = jnp.exp(scores - peak)
                total = jnp.sum(terms, axis=1, keepdims=True)
                probs.append((terms * (1.0 / total)).astype(bf16))
            context = mm(probs[0], v * head_lanes(0)) + mm(probs[1], v * head_lanes(1))
            turned = [mm(probs[a], r.flip[...]).astype(bf16) for a in range(2)]
            turned_t = [jnp.transpose(turned[a]) for a in range(2)]
            for a in range(2):
                r.probs[2 * p + a, rows, :] = turned[a]
                r.probs_t[2 * p + a, rows, :] = turned_t[a]
            r.ctx[rows, cols] = context.astype(bf16)

    loop(H // 2, pair)


def out_project(r):
    ctx = r.ctx[...]
    u = mm_t(r.attn_qt[...], ctx)
    r.u_t[3 * R :, :] = u[3 * R :, :]
    mixed_t = (u * r.lam_col[...] * rank_group(3)).astype(bf16)
    r.hidden[...] = (
        mm(ctx, whole(r.wout))
        + r.attn_bias[3:4, :].astype(f32)
        + tmm(mixed_t, r.attn_pt[...])
    )
    gain, bias = r.norm_gain[0:1, :].astype(f32), r.norm_bias[0:1, :].astype(f32)

    def part(i):
        rows = block(i, 128)
        total = r.tok[rows, :].astype(f32) + r.hidden[rows, :]
        centre = total - mean_row(total)
        rs = lax.rsqrt(mean_row(centre * centre) + EPS)
        xhat = centre * rs
        hidden = xhat * gain + bias
        r.xhat1[rows, :] = xhat
        r.rs1[rows, :] = rs
        r.hidden[rows, :] = hidden
        r.hid[rows, :] = hidden.astype(bf16)

    loop(L // 128, part)
    r.u_up_t[...] = mm_t(r.up_qt[...], r.hid[...])


UP_BLOCK = 512


def up_project(r, before=None):
    def part(i):
        if before is not None:
            before(i)
        up_block(r, i)

    loop(FF // UP_BLOCK, part)


def up_block(r, i):
    mixed_t = (r.u_up_t[...] * as_column(r.lam[4:5, :])).astype(bf16)
    cols = block(i, UP_BLOCK)
    pre = (
        mm(r.hid[...], columns(r.wup, cols))
        + r.up_bias[:, cols].astype(f32)
        + tmm(mixed_t, r.up_pt[:, cols])
    )
    phi = 0.5 * (1.0 + lax.erf(pre * np.float32(np.sqrt(0.5))))
    r.act[:, cols] = (pre * phi).astype(bf16)
    bell = jnp.exp(-0.5 * pre * pre) * np.float32(1.0 / np.sqrt(2.0 * np.pi))
    r.slope[:, cols] = (phi + pre * bell).astype(bf16)


def down_reduce(r):
    r.u_down_t[...] = mm_t(r.down_qt[...], r.act[...])


def down_project(r):
    mixed_t = (r.u_down_t[...] * as_column(r.lam[5:6, :])).astype(bf16)
    r.branch[...] = (
        mm_t(r.act[...], whole(r.wdown))
        + r.down_bias[...].astype(f32)
        + tmm(mixed_t, r.down_pt[...])
    )


def norm_two(r):
    gain, bias = r.norm_gain[1:2, :].astype(f32), r.norm_bias[1:2, :].astype(f32)

    def part(i):
        rows = block(i, 128)
        total = r.hidden[rows, :] + r.branch[rows, :]
        centre = total - mean_row(total)
        rs = lax.rsqrt(mean_row(centre * centre) + EPS)
        xhat = centre * rs
        r.low_out[rows, :] = (xhat * gain + bias).astype(bf16)
        e = r.cot[rows, :].astype(f32) * gain
        grad = rs * (e - mean_row(e) - xhat * mean_row(e * xhat))
        r.gsum2[rows, :] = grad
        r.gb5[rows, :] = grad.astype(bf16)

    loop(L // 128, part)


def back_factors(gb, p_t, u_t, lam):
    dmixed = mm_t(p_t, gb)
    return mm((u_t * lam).astype(bf16), gb), (dmixed * lam).astype(bf16), dmixed * u_t


def as_row(column):
    return jnp.transpose(jnp.broadcast_to(column, (column.shape[0], 128)))[0:1, :]


BACK_BLOCK = 1024


def down_back(r):
    gb = r.gb5[...]
    dp, du, dlam = back_factors(gb, r.down_pt[...], r.u_down_t[...], as_column(r.lam[5:6, :]))
    r.grad_narrow[R:, :] = dp
    r.grad_lam[5:6, 0:R] = as_row(jnp.sum(dlam, axis=1, keepdims=True))[:, 0:R]

    def part(i):
        cols = block(i, BACK_BLOCK)
        grad = mm(gb, columns(r.wdown, cols)) + tmm(du, r.down_qt[:, cols])
        r.grad_wide[R:, cols] = mm(du, r.act[:, cols])
        r.gpre[:, cols] = (grad * r.slope[:, cols].astype(f32)).astype(bf16)

    loop(FF // BACK_BLOCK, part)


def up_back(r):
    gb = r.gpre[...]
    dp, du, dlam = back_factors(gb, r.up_pt[...], r.u_up_t[...], as_column(r.lam[4:5, :]))
    r.grad_wide[:R, :] = dp
    r.grad_lam[4:5, 0:R] = as_row(jnp.sum(dlam, axis=1, keepdims=True))[:, 0:R]
    r.grad_narrow[:R, :] = mm(du, r.hid[...])
    r.branch[...] = mm_t(gb, whole(r.wup)) + tmm(du, r.up_qt[...])
    gain = r.norm_gain[0:1, :].astype(f32)

    def part(i):
        rows = block(i, 128)
        e = (r.gsum2[rows, :] + r.branch[rows, :]) * gain
        xhat = r.xhat1[rows, :]
        grad = r.rs1[rows, :] * (e - mean_row(e) - xhat * mean_row(e * xhat))
        r.gsum1[rows, :] = grad
        r.gb3[rows, :] = grad.astype(bf16)

    loop(L // 128, part)


def out_back(r):
    gb = r.gb3[...]
    dp, du, dlam = back_factors(gb, r.attn_pt[...], r.u_t[...], r.lam_col[...] * rank_group(3))
    r.grad_fourth[:R, :] = dp[3 * R :, :]
    r.grad_fourth[R:, :] = mm(du, r.ctx[...])[3 * R :, :]
    r.grad_lam[0:1, 0 : 4 * R] = as_row(jnp.sum(dlam * rank_group(3), axis=1, keepdims=True))
    r.gctx[...] = (mm_t(gb, whole(r.wout)) + tmm(du, r.attn_qt[...])).astype(bf16)
    r.g_t[...] = jnp.transpose(r.gctx[...])


def attend_back(r, before=None):
    def pair(p):
        if before is not None:
            before(p)
        cols = block(p, 2 * DH)
        low = iota((HALF, HALF), 1) >= iota((HALF, HALF), 0)
        zero = jnp.zeros((HALF, HALF), bf16)
        units = [(a, b) for a in range(2) for b in range(2)]
        part = [slice(HALF * b, HALF * (b + 1)) for b in range(2)]
        feats = [block(2 * p + a, DH) for a in range(2)]
        ready, stores = {}, []
        for a, b in units:
            rows, head, lanes = part[b], 2 * p + a, head_lanes(a)
            gprobs = mm(r.gctx[rows, cols] * lanes, r.v_rev_t[cols, rows])
            gprobs_t = mm(r.v_rev[rows, cols] * lanes, r.g_t[cols, rows])
            probs = r.probs[head, rows, :].astype(f32)
            delta = jnp.sum(probs * gprobs, axis=1, keepdims=True)
            gs = (probs * (gprobs - delta)).astype(bf16)
            probs_t = r.probs_t[head, rows, :].astype(f32)
            delta_t = jnp.sum(probs_t * gprobs_t, axis=0, keepdims=True)
            gs_t = (probs_t * (gprobs_t - delta_t)).astype(bf16)
            ready[a, b] = gs, gs_t
        for a in range(2):
            gpk = gpq = None
            for b in range(2):
                rows = part[b]
                gs, gs_t = ready[a, b]
                turn = pltpu.roll(gs, 0, 1, stride=1, stride_axis=0)
                to = jnp.concatenate([jnp.where(low, turn, zero), jnp.where(low, zero, turn)], axis=1)
                turn_t = pltpu.roll(gs_t, 0, 1, stride=1, stride_axis=0)
                fro = jnp.concatenate([jnp.where(low, turn_t, zero), jnp.where(low, zero, turn_t)], axis=1)
                queries, keys = r.qt[feats[a], rows], r.k_rev_t[feats[a], rows]
                gq = mm(keys, gs_t) + mm_t(r.pk_far_t[feats[a], :], to)
                gk = mm(queries, gs) + mm_t(r.pq_far_t[feats[a], :], fro)
                gv = mm(r.g_t[feats[a], rows], r.probs[2 * p + a, rows, :])
                gpk_b, gpq_b = mm(queries, to), mm(keys, fro)
                gpk = gpk_b if gpk is None else gpk + gpk_b
                gpq = gpq_b if gpq is None else gpq + gpq_b
                stores.append((r.gq_t, feats[a], rows, gq * SCALE))
                stores.append((r.gk_t, feats[a], rows, gk * SCALE))
                stores.append((r.gv_t, feats[a], rows, gv))
            stores.append((r.gpk_t, feats[a], slice(None), gpk * SCALE))
            stores.append((r.gpq_t, feats[a], slice(None), gpq * SCALE))
        for ref, feat, rows, value in stores:
            ref[feat, rows] = value.astype(bf16)

    loop(H // 2, pair)


def qkv_factors(r):
    flip_columns(r, r.gk_t, r.gk_t)
    flip_columns(r, r.gv_t, r.gv_t)
    lam = r.lam_col[...]
    u = r.u_t[...]
    dmixed = jnp.zeros((4 * R, L), f32)
    ap = jnp.zeros((4 * R, D), f32)
    for n, g in ((0, r.gq_t), (1, r.gk_t), (2, r.gv_t)):
        gb = g[...]
        dmixed += mm(r.attn_pt[...], gb) * rank_group(n)
        ap += mm_t((u * lam * rank_group(n)).astype(bf16), gb)
    du = (dmixed * lam).astype(bf16)
    r.du_t[...] = du
    aq = mm(du, r.tok[...])
    lam_grad = dmixed * u
    u = r.u_pos_t[...]
    for n, grads in ((0, r.gpq_t), (1, r.gpk_t)):
        gb = grads[...]
        dmixed = mm(r.attn_pt[...], gb) * rank_group(n)
        ap += mm_t((u * lam * rank_group(n)).astype(bf16), gb)
        aq += mm((dmixed * lam).astype(bf16), r.emb_far[...])
        lam_grad += dmixed * u
    r.grad_attn[: 3 * R, :] = ap[: 3 * R, :]
    r.grad_attn[3 * R :, :] = aq[: 3 * R, :]
    r.grad_lam[0:1, 0 : 4 * R] += as_row(jnp.sum(lam_grad, axis=1, keepdims=True))


def qkv_input(r):
    grad_t = tmm(r.attn_qt[...], r.du_t[...])
    for n, g in ((0, r.gq_t), (1, r.gk_t), (2, r.gv_t)):
        grad_t += mm(whole(r.wqkv.at[n]), g[...])
    r.gsum1[...] += jnp.transpose(grad_t)


def finish_layer(r):
    r.layer_out[...] = mm(r.unshift[...], r.low_out[...]).astype(bf16)


def finish_grad(r):
    r.grad_tokens[...] = mm(r.unshift[...], r.gsum1[...].astype(bf16)).astype(bf16)


MESH = pl.DeviceIdType.MESH
SLOTS = 6
ALL = slice(None)
WIDTH = dict(wqkv=384, wout=384, wup=1536, wdown=1536, embed=384)


class Gather:
    def __init__(self, r):
        self.r, self.parts = r, PARTS
        group = lax.axis_index("group")
        self.x = lax.axis_index("inner")
        self.z, self.y, self.c = group // 4, (group // 2) % 2, group % 2

    def device(self, x=None, y=None, z=None, c=None):
        x = self.x if x is None else x
        y = self.y if y is None else y
        z = self.z if z is None else z
        c = self.c if c is None else c
        return ((z * 2 + y) * 2 + c, x)

    def greet(self):
        barrier = pltpu.get_barrier_semaphore()
        partners = [self.device(x=1 - self.x), self.device(y=1 - self.y), self.device(c=1 - self.c)]
        partners += [self.device(z=(self.z + j) % 4) for j in (1, 2, 3)]
        for partner in partners:
            pl.semaphore_signal(barrier, inc=1, device_id=partner, device_id_type=MESH)
        pl.semaphore_wait(barrier, len(partners))

    def region(self, p, z, y, c, x):
        name, lead, start, count, _ = self.parts[p]
        ref = getattr(self.r, name)
        ref = ref if lead is None else ref.at[lead]
        width = WIDTH[name]
        cols = ALL if x is None else pl.ds(pl.multiple_of(x * width, 128), width)
        return ref.at[z, y, c, pl.ds(start, count), cols]

    def shard(self, p):
        name, lead, start, count, _ = self.parts[p]
        ref = getattr(self.r, name + "_shard")
        ref = ref if lead is None else ref.at[lead]
        return ref.at[pl.ds(start, count), :]

    def remote(self, source, target, p, slot, device):
        return pltpu.make_async_remote_copy(
            source,
            target,
            self.r.send_sem.at[p, slot],
            self.r.recv_sem.at[p, slot],
            device_id=device,
            device_id_type=MESH,
        )

    def place_own(self, p):
        target = self.region(p, self.z, self.y, self.c, self.x)
        return pltpu.make_async_copy(self.shard(p), target, self.r.local_sem.at[p])

    def held(self, p, done, c):
        z = ALL if "z" in done else self.z
        y = ALL if "y" in done else self.y
        return self.region(p, z, y, c, None if "x" in done else self.x)

    def outgoing(self, p, k, own=None):
        route = self.parts[p][4]
        region = self.held(p, route[:k], self.c)
        source = region if own is None else own
        if route[k] == "z":
            devices = [self.device(z=(self.z + j) % 4) for j in (1, 2, 3)]
        else:
            devices = [self.device(y=1 - self.y) if route[k] == "y" else self.device(x=1 - self.x)]
        return [self.remote(source, region, p, k, device) for device in devices]

    def arriving(self, p, k, c):
        route = self.parts[p][4]
        done = route[:k]
        z = ALL if "z" in done else self.z
        y = ALL if "y" in done else self.y
        x = None if "x" in done else self.x
        if route[k] == "z":
            return [self.region(p, (self.z + j) % 4, y, c, x) for j in (1, 2, 3)]
        if route[k] == "y":
            return [self.region(p, z, 1 - self.y, c, x)]
        return [self.region(p, z, y, c, 1 - self.x)]

    def amount(self, p, k):
        route = self.parts[p][4]
        if route[k] != "z":
            return self.held(p, route[:k], self.c)
        y = ALL if "y" in route[:k] else self.y
        return self.region(p, pl.ds(0, 3), y, self.c, None if "x" in route[:k] else self.x)

    def sibling(self, p, k, c):
        regions = [self.held(p, self.parts[p][4][:1], c)] if k == 0 else self.arriving(p, k, c)
        device = self.device(c=1 - self.c)
        return [self.remote(ref, ref, p, 3 + k, device) for ref in regions]

    def sibling_amount(self, p, k):
        ref = self.held(p, self.parts[p][4][:1], self.c) if k == 0 else self.amount(p, k)
        return self.remote(ref, ref, p, 3 + k, self.device(c=1 - self.c))

    def start(self, copies):
        for copy in copies:
            copy.start()

    def begin(self, p):
        self.place_own(p).start()
        self.start(self.outgoing(p, 0, self.shard(p)))

    def event(self, p, k):
        self.stage_amount(p, k).wait_recv()
        if k == 0:
            self.place_own(p).wait()
        if k < 2:
            self.start(self.outgoing(p, k + 1))
        self.start(self.sibling(p, k, self.c))

    def stage_amount(self, p, k):
        ref = self.amount(p, k)
        return self.remote(ref, ref, p, k, self.device(c=1 - self.c))

    def ready(self, p):
        for k in range(3):
            self.sibling_amount(p, k).wait_recv()

    def drain(self):
        for p in range(len(self.parts)):
            for k in range(3):
                self.stage_amount(p, k).wait_send()
                self.sibling_amount(p, k).wait_send()


class Exchange:
    def __init__(self, r, comm, name, index):
        self.comm, self.index = comm, index
        self.pack = getattr(r, "pack_" + name)
        self.swap = getattr(r, "swap_" + name)
        self.mine = getattr(r, "mine_" + name)
        self.terms = getattr(r, "terms_" + name)
        self.sums = getattr(r, "sums_" + name)
        self.send_sem, self.recv_sem = r.sum_send, r.sum_recv
        self.chip = comm.z * 2 + comm.y

    def remote(self, source, target, stage, device):
        return pltpu.make_async_remote_copy(
            source,
            target,
            self.send_sem.at[self.index, stage],
            self.recv_sem.at[self.index, stage],
            device_id=device,
            device_id_type=MESH,
        )

    def fill(self, sources):
        count = self.pack.shape[3]
        tile = 0
        for ref, width in sources:
            for row in range(ref.shape[0] // 8):
                for col in range(width // 128):
                    core, chip, slot = tile // (8 * count), tile // count % 8, tile % count
                    for x in range(2):
                        start = (x * width if ref.shape[1] > width else 0) + 128 * col
                        self.pack[x, core, chip, slot] = ref[8 * row : 8 * row + 8, start : start + 128]
                    tile += 1
        while tile < 16 * count:
            core, chip, slot = tile // (8 * count), tile // count % 8, tile % count
            for x in range(2):
                self.pack[x, core, chip, slot] = jnp.zeros((8, 128), f32)
            tile += 1

    def swap_copy(self):
        c = self.comm.c
        return self.remote(self.pack.at[:, 1 - c], self.swap, 0, self.comm.device(c=1 - c))

    def chip_copies(self):
        own = self.comm.x * 8 + self.chip
        for j in range(1, 16):
            index = (own + j) % 16
            x, chip = index // 8, index % 8
            yield self.remote(self.mine.at[x, chip], self.terms.at[own], 1, (chip * 2 + self.comm.c, x))

    def sum_copies(self):
        own = self.chip * 2 + self.comm.c
        slot = self.sums.at[own]
        for j in range(1, 16):
            yield self.remote(slot, slot, 2, ((own + j) % 16, self.comm.x))

    def all_copies(self, stage):
        ref = (self.terms if stage == 1 else self.sums).at[pl.ds(0, 15)]
        return self.remote(ref, ref, stage, self.comm.device(c=1 - self.comm.c))

    def start(self, sources):
        self.fill(sources)
        self.swap_copy().start()

    def spread(self):
        self.swap_copy().wait_recv()
        comm = self.comm
        for x in range(2):
            self.mine[x] = self.pack[x, comm.c] + self.swap[x]
        for copy in self.chip_copies():
            copy.start()
        self.terms[comm.x * 8 + self.chip] = self.mine[comm.x, self.chip]

    def add(self):
        self.all_copies(1).wait_recv()
        total = self.terms[0]
        for index in range(1, 16):
            total = total + self.terms[index]
        self.sums[self.chip * 2 + self.comm.c] = total
        for copy in self.sum_copies():
            copy.start()

    def collect(self):
        self.all_copies(2).wait_recv()

    def drain(self):
        self.swap_copy().wait_send()
        self.all_copies(1).wait_send()
        self.all_copies(2).wait_send()


def exchange_scratch(name, count):
    tiles = (count, 8, 128)
    return {
        "pack_" + name: ((2, 2, 8) + tiles, f32),
        "swap_" + name: ((2, 8) + tiles, f32),
        "mine_" + name: ((2, 8) + tiles, f32),
        "terms_" + name: ((16,) + tiles, f32),
    }


PARTS = (
    ("embed", None, 0, 32, "zxy"),
    ("wqkv", 0, 0, 48, "zyx"),
    ("wqkv", 1, 0, 48, "zxy"),
    ("wqkv", 2, 0, 48, "zyx"),
    ("wout", None, 0, 48, "zyx"),
    ("wup", None, 0, 16, "zxy"),
    ("wup", None, 16, 16, "xzy"),
    ("wup", None, 32, 16, "zyx"),
    ("wdown", None, 0, 16, "zyx"),
    ("wdown", None, 16, 16, "xyz"),
    ("wdown", None, 32, 16, "zxy"),
)
PLAN = (
    ("b", 0),
    ("b", 1),
    ("b", 2),
    ("b", 3),
    ("b", 4),
    ("b", 5),
    ("b", 6),
    ("b", 7),
    ("b", 8),
    ("b", 9),
    ("b", 10),
    ("s", "prep0"),
    ("s", "prep1"),
    (0, 6),
    (0, 9),
    (0, 0),
    (0, 1),
    (1, 9),
    (1, 0),
    (0, 2),
    (1, 1),
    (0, 3),
    (1, 2),
    (0, 4),
    (2, 0),
    ("s", "pos0"),
    (1, 3),
    (0, 5),
    (2, 1),
    ("s", "pos1"),
    (0, 7),
    (2, 2),
    ("s", "pos2"),
    ("s", "pos3"),
    (2, 3),
    (0, 8),
    (1, 4),
    ("s", "qkv0"),
    ("s", "qkv1"),
    ("s", "qkv2"),
    ("s", "qkv3"),
    (1, 5),
    (0, 10),
    (1, 7),
    ("s", "qkv4"),
    ("s", "attend0.0"),
    ("s", "attend0.1"),
    ("s", "attend1.0"),
    (1, 8),
    ("s", "attend1.1"),
    (2, 4),
    ("s", "attend2.0"),
    (1, 6),
    ("s", "attend2.1"),
    ("s", "attend3.0"),
    (1, 10),
    ("s", "attend3.1"),
    (2, 5),
    ("s", "attend4.0"),
    ("s", "attend4.1"),
    ("s", "attend5.0"),
    ("s", "attend5.1"),
    ("s", "out"),
    (2, 7),
    (2, 6),
    ("s", "up0"),
    ("s", "up1"),
    (2, 9),
    ("s", "up2"),
    ("s", "up3"),
    (2, 8),
    ("s", "up4"),
    ("s", "up5"),
    ("s", "down0"),
    (2, 10),
    ("s", "down1"),
)


STEPS = dict(
    prep0=(prepare_masks, ()),
    prep1=(prepare_factors, ()),
    pos0=(embed_positions, ("embed",)),
    pos1=(functools.partial(project_position, 0, False, "pq_far_t"), (("wqkv", 0),)),
    pos2=(functools.partial(project_position, 1, True, "pk_near_t"), (("wqkv", 1),)),
    pos3=(functools.partial(project_position, 1, False, "pk_far_t"), ()),
    qkv0=(reduce_tokens, ()),
    qkv1=(functools.partial(project_token, 0, "q"), ()),
    qkv2=(functools.partial(project_token, 1, "k"), ()),
    qkv3=(functools.partial(project_token, 2, "v"), (("wqkv", 2),)),
    qkv4=(arrange_heads, ()),
    attend=(attend, ()),
    out=(out_project, ("wout",)),
    up=(up_project, ("wup",)),
    down0=(down_reduce, ()),
    down1=(down_project, ("wdown",)),
)
BACKWARD = (
    norm_two,
    down_back,
    up_back,
    out_back,
)


def run_plan(r, comm, plan):
    ready = set()
    waiting = []
    turns = {}
    counts = dict(attend=H, up=FF // UP_BLOCK)

    def moves(items):
        for move in items:
            comm.event(*move)

    def before(*turn):
        for place, items in turns.items():
            if items and place[1:] == turn[1:]:
                pl.when(turn[0] == place[0])(functools.partial(moves, items))

    for kind, arg in plan:
        if kind == "b":
            comm.begin(arg)
            continue
        if kind != "s":
            waiting.append((arg, kind))
            continue
        name = arg.rstrip("0123456789.")
        looped = name in counts
        step, needs = STEPS[name if looped else arg]
        if not looped or not turns:
            moves(waiting)
            waiting = []
            for p, part in enumerate(comm.parts):
                if p not in ready and (part[0] in needs or part[:2] in needs):
                    comm.ready(p)
                    ready.add(p)
        if not looped:
            step(r)
            continue
        turns[tuple(int(c) for c in arg[len(name) :].split("."))] = waiting
        waiting = []
        if len(turns) == counts[name]:
            step(r, before)
            turns = {}
    moves(waiting)


EARLY, LATE = 4, 2
SUMS = dict(sums_early=((16, EARLY, 8, 128), f32), sums_late=((16, LATE, 8, 128), f32))
FUSED_SCRATCH = {
    **SCRATCH,
    **GATHERED,
    **GRADS,
    **exchange_scratch("early", EARLY),
    **exchange_scratch("late", LATE),
}


def layer_kernel(fused, *refs):
    r = Refs()
    if fused:
        names = INPUTS + SHARDS + OUTPUTS + list(SUMS) + list(FUSED_SCRATCH)
        names += ["load_sem", "send_sem", "recv_sem", "local_sem", "sum_send", "sum_recv"]
    else:
        names = INPUTS + list(GATHERED) + OUTPUTS + list(GRADS) + list(SCRATCH) + ["load_sem"]
    for name, ref in zip(names, refs, strict=True):
        setattr(r, name, ref)
    for name, target in ALIASES.items():
        setattr(r, name, getattr(r, target))
    if not fused:
        r.grad_lam[...] = jnp.zeros_like(r.grad_lam)
        for step, _ in STEPS.values():
            step(r)
        for step in BACKWARD + (attend_back, qkv_factors, qkv_input, finish_layer, finish_grad):
            step(r)
        return

    comm = Gather(r)
    comm.greet()
    r.grad_lam[...] = jnp.zeros_like(r.grad_lam)
    run_plan(r, comm, PLAN)
    for step in BACKWARD:
        step(r)
    early = Exchange(r, comm, "early", 0)
    late = Exchange(r, comm, "late", 1)
    early.start(((r.grad_wide, FF // 2), (r.grad_narrow, D // 2), (r.grad_fourth, D // 2)))

    def before(p):
        pl.when(p == 1)(early.spread)
        pl.when(p == 3)(early.add)

    attend_back(r, before)
    qkv_factors(r)
    late.start(((r.grad_attn, D // 2), (r.grad_lam, 128)))
    finish_layer(r)
    late.spread()
    qkv_input(r)
    finish_grad(r)
    comm.drain()
    early.collect()
    early.drain()
    late.add()
    late.collect()
    late.drain()


OUT_SHAPES = dict(layer_out=((L, D), bf16), grad_tokens=((L, D), bf16), **SUMS, **GRADS)


def unpack_kernel(layer_in, grad_in, early, late, layer_out, grad_out, ap, aq, upp, upq, dnp, dnq, glam, *parts):
    layer_out[...] = layer_in[...]
    grad_out[...] = grad_in[...]
    wide, narrow, fourth, attn = parts
    for sums, refs in ((early, (wide, narrow, fourth)), (late, (attn,))):
        count = sums.shape[1]
        tile = 0
        for ref in refs:
            for row in range(ref.shape[0] // 8):
                for col in range(ref.shape[1] // 128):
                    core, chip, slot = tile // (8 * count), tile // count % 8, tile % count
                    ref[8 * row : 8 * row + 8, 128 * col : 128 * col + 128] = sums[chip * 2 + core, slot]
                    tile += 1
    core, chip, slot = tile // (8 * count), tile // count % 8, tile % count
    lam = sums[chip * 2 + core, slot]
    for n in range(4):
        glam[n : n + 1, :] = lam[0:1, R * n : R * (n + 1)]
    glam[4:6, :] = lam[4:6, 0:R]
    upp[...] = wide[:R, :]
    dnq[...] = wide[R:, :]
    upq[...] = narrow[:R, :]
    dnp[...] = narrow[R:, :]
    for n in range(3):
        ap[:, n, :] = attn[R * n : R * (n + 1), :]
        aq[:, n, :] = attn[3 * R + R * n : 3 * R + R * (n + 1), :]
    ap[:, 3, :] = fourth[:R, :]
    aq[:, 3, :] = fourth[R:, :]


def unpack_call(layer_out, grad_tokens, early, late):
    half = D // 2
    vmem = pl.BlockSpec(memory_space=pltpu.VMEM)
    shapes = [
        ((L, D), bf16),
        ((L, D), bf16),
        ((R, 4, half), f32),
        ((R, 4, half), f32),
        ((R, FF // 2), f32),
        ((R, half), f32),
        ((R, half), f32),
        ((R, FF // 2), f32),
        ((6, R), f32),
    ]
    return pl.pallas_call(
        unpack_kernel,
        out_shape=[jax.ShapeDtypeStruct(*shape) for shape in shapes],
        in_specs=[vmem] * 4,
        out_specs=[vmem] * len(shapes),
        scratch_shapes=[
            pltpu.VMEM((2 * R, FF // 2), f32),
            pltpu.VMEM((2 * R, half), f32),
            pltpu.VMEM((2 * R, half), f32),
            pltpu.VMEM((6 * R, half), f32),
        ],
    )(layer_out, grad_tokens, early, late)


def layer_call(args, weights, fused):
    vmem = pl.BlockSpec(memory_space=pltpu.VMEM)
    hbm = pl.BlockSpec(memory_space=pl.ANY)
    load_sem = pltpu.SemaphoreType.DMA((2,))
    if fused:
        outputs = OUTPUTS + list(SUMS)
        scratch = [pltpu.VMEM(*spec) for spec in FUSED_SCRATCH.values()] + [
            load_sem,
            pltpu.SemaphoreType.DMA((len(PARTS), SLOTS)),
            pltpu.SemaphoreType.DMA((len(PARTS), SLOTS)),
            pltpu.SemaphoreType.DMA((len(PARTS),)),
            pltpu.SemaphoreType.DMA((2, 3)),
            pltpu.SemaphoreType.DMA((2, 3)),
        ]
        extra = dict(collective_id=0, has_side_effects=True)
    else:
        outputs = OUTPUTS + list(GRADS)
        scratch = [pltpu.VMEM(*spec) for spec in SCRATCH.values()] + [load_sem]
        weights = [w.reshape(GATHERED[name][0]) for name, w in zip(GATHERED, weights)]
        extra = {}
    return pl.pallas_call(
        functools.partial(layer_kernel, fused),
        out_shape=[jax.ShapeDtypeStruct(*OUT_SHAPES[name]) for name in outputs],
        in_specs=[hbm if name in IN_HBM else vmem for name in INPUTS]
        + [hbm if fused else vmem] * len(weights),
        out_specs=[vmem] * len(outputs),
        scratch_shapes=scratch,
        compiler_params=pltpu.CompilerParams(vmem_limit_bytes=63 * 2**20, **extra),
    )(*args, *weights)


def gather_plain(w_qkv, w_out, w_up, down_t, rel_embed):
    parts = []
    for shard, rows, cols in (
        (w_qkv, 1, 2),
        (w_out, 0, 1),
        (w_up, 0, 1),
        (down_t, 0, 1),
        (rel_embed, 0, 1),
    ):
        part = lax.all_gather(shard, "inner", axis=cols, tiled=True)
        parts.append(lax.all_gather(part, "group", axis=rows, tiled=True))
    return parts


def reduce_plain(grads):
    shared = [
        lax.psum(lax.psum_scatter(g, "inner", scatter_dimension=1, tiled=True), "group")
        for g in grads[:-1]
    ]
    return shared, lax.psum(grads[-1], ("group", "inner"))


def on_device(
    tokens,
    cotangent,
    segments,
    w_qkv,
    w_out,
    w_up,
    w_down,
    rel_embed,
    attn_bias,
    up_bias,
    down_bias,
    norm_gain,
    norm_bias,
    attn_p,
    attn_q,
    up_p,
    up_q,
    down_p,
    down_q,
    lam,
):
    fused = (lax.axis_size("group"), lax.axis_size("inner")) == (16, 2)
    down_t = jnp.transpose(w_down)
    weights = (w_qkv, w_out, w_up, down_t, rel_embed)
    if not fused:
        weights = gather_plain(*weights)
    args = (
        tokens,
        cotangent,
        segments,
        jnp.asarray(bucket_rows()),
        attn_bias,
        up_bias[None],
        down_bias[None],
        norm_gain,
        norm_bias,
        jnp.transpose(attn_p, (2, 1, 0)),
        jnp.transpose(attn_q, (2, 1, 0)),
        up_p.T,
        up_q.T,
        down_p.T,
        down_q.T,
        lam,
    )
    layer_out, grad_tokens, *sums = layer_call(args, weights, fused)
    if fused:
        layer_out, grad_tokens, ap, aq, upp, upq, dnp, dnq, grad_lam = unpack_call(
            layer_out, grad_tokens, *sums
        )
    else:
        (wide, narrow, fourth, attn), lam_sums = reduce_plain(sums)
        by_rank = [attn[R * n : R * (n + 1)] for n in range(6)]
        ap = jnp.stack(by_rank[:3] + [fourth[:R]], axis=1)
        aq = jnp.stack(by_rank[3:] + [fourth[R:]], axis=1)
        upp, dnq, upq, dnp = wide[:R], wide[R:], narrow[:R], narrow[R:]
        grad_lam = jnp.concatenate([lam_sums[0, : 4 * R].reshape(4, R), lam_sums[4:6, :R]], axis=0)
    return (
        layer_out,
        grad_tokens,
        jnp.transpose(ap, (2, 1, 0)),
        jnp.transpose(aq, (2, 1, 0)),
        upp.T,
        upq.T,
        dnp.T,
        dnq.T,
        grad_lam,
    )


def solution(mesh):
    rows = P(("group", "inner"), None)
    return jax.shard_map(
        on_device,
        mesh=mesh,
        in_specs=(
            rows,
            rows,
            rows,
            P(None, "group", "inner"),
            P("group", "inner"),
            P("group", "inner"),
            P("inner", "group"),
            P("group", "inner"),
        )
        + (P(),) * 12,
        out_specs=(
            rows,
            rows,
            P("inner", None, None),
            P("inner", None, None),
            P("inner", None),
            P("inner", None),
            P("inner", None),
            P("inner", None),
            P(),
        ),
        check_vma=False,
    )
```

profile of v0, /device:TPU:0, one launch (start us, length us, event | category | flops | bytes accessed | tf_op | source)
XLA Modules:
  0.0 144.0 jit_solution(2256809426320603029)
XLA Ops:
  0.6 0.0 copy-start.1
  0.7 0.0 copy-start
  0.7 0.7 copy-done.1
  1.3 0.6 broadcast_in_dim.7.refs_6_
  1.9 0.0 copy-done
  1.9 0.6 broadcast_in_dim.6.refs_5_
  2.5 138.7 %shard_map.268 = (bf16[512,768]{1,0:T(8,128)(2,1)}, bf16[512,768]{1,0:T(8,128)(2,1)}, f32[16,4,8,128]{3,2,1,0:T(8,128)}, f32[16,2,8,128]{3,2,1,0:T(8,128)}) custom-call(bf16[512,768]{1,0:T(8,128)(2,1)} %refs_0_.1, bf16[512,768]{1,0:T(8,128)(2,1)} %refs_1_.1, s32[1,512]{1,0:T(1,128)} %refs_2_.1, s32[2,512]{1,0:T(2,128)} %constant.2.clone.refs_3_, ...), custom_call_target="tpu_custom_call" | custom-call | tf_op jit(solution)/shard_map/pallas_call | solution.py:1098
  141.2 2.8 %shard_map.269 = (bf16[512,768]{1,0:T(8,128)(2,1)}, bf16[512,768]{1,0:T(8,128)(2,1)}, f32[12,4,384]{2,1,0:T(4,128)}, f32[12,4,384]{2,1,0:T(4,128)}, f32[12,1536]...) custom-call(bf16[512,768]{1,0:T(8,128)(2,1)} %get-tuple-element.22.layer_in, ...), custom_call_target="tpu_custom_call" | custom-call | tf_op jit(solution)/shard_map/pallas_call | solution.py:1064
Async XLA Ops:
  0.6 0.7 copy-start.1
  0.7 1.3 copy-start
where the time goes:
time: 144 us
  Pallas kernels  141 us (98%)
  local copies, waits for them, and re-layouts  1.86 us (1%)
    pallas_call x1, Pallas kernels, layer_call(): pl.pallas_call(functools.partial(layer_kernel, fused), out_shape=[jax.Sha...  139 us

commit v1 on v0

--- a/solution.py
+++ b/solution.py
@@ -75,13 +75,23 @@
     return jnp.sum(values, axis=1, keepdims=True) * (1.0 / D)
 
 
+def flat(block):
+    return block.reshape(-1, block.shape[-1])
+
+
 def whole(ref):
-    return ref[...].reshape(-1, ref.shape[-1])
-
-
-def columns(ref, cols):
-    picked = ref[:, :, :, :, cols]
-    return picked.reshape(-1, picked.shape[-1])
+    return jnp.concatenate([flat(ref[x]) for x in range(2)], axis=1)
+
+
+THIRD = FF // 6
+
+
+def whole_wide(ref):
+    return jnp.concatenate([flat(ref[t, x]) for x in range(2) for t in range(3)], axis=1)
+
+
+def third(t, x):
+    return pl.ds(pl.multiple_of((3 * x + t) * THIRD, THIRD), THIRD)
 
 
 SCRATCH = dict(
@@ -116,6 +126,8 @@
     down_qt=((R, FF), bf16),
     lam_row=((8, 4 * R), f32),
     lam_col=((4 * R, 1), f32),
+    up_row=((1, FF), f32),
+    down_row=((1, D), f32),
     u_t=((4 * R, L), f32),
     du_t=((4 * R, L), bf16),
     u_pos_t=((4 * R, L), f32),
@@ -135,11 +147,11 @@
 )
 
 GATHERED = dict(
-    wqkv=((3, 4, 2, 2, 48, D), bf16),
-    wout=((4, 2, 2, 48, D), bf16),
-    wup=((4, 2, 2, 48, FF), bf16),
-    wdown=((4, 2, 2, 48, FF), bf16),
-    embed=((4, 2, 2, 32, D), bf16),
+    wqkv=((3, 2, 4, 2, 2, 48, D // 2), bf16),
+    wout=((2, 4, 2, 2, 48, D // 2), bf16),
+    wup=((3, 2, 4, 2, 2, 48, THIRD), bf16),
+    wdown=((3, 2, 4, 2, 2, 48, THIRD), bf16),
+    embed=((2, 4, 2, 2, 32, D // 2), bf16),
 )
 
 ALIASES = dict(
@@ -235,6 +247,8 @@
     for n in range(4):
         r.lam_row[0:1, R * n : R * (n + 1)] = r.lam[n : n + 1, :]
     r.lam_col[...] = as_column(r.lam_row[0:1, :])
+    r.up_row[...] = r.up_bias[...].astype(f32).reshape(1, FF)
+    r.down_row[...] = r.down_bias[...].astype(f32).reshape(1, D)
     copies[0].wait()
     r.tok[...] = mm(r.shift[...], r.tok[...]).astype(bf16)
     copies[1].wait()
@@ -359,24 +373,21 @@
     r.u_up_t[...] = mm_t(r.up_qt[...], r.hid[...])
 
 
-UP_BLOCK = 512
-
-
 def up_project(r, before=None):
     def part(i):
         if before is not None:
             before(i)
-        up_block(r, i)
-
-    loop(FF // UP_BLOCK, part)
-
-
-def up_block(r, i):
+        up_block(r, i // 2, i % 2)
+
+    loop(6, part)
+
+
+def up_block(r, t, x):
+    cols = third(t, x)
     mixed_t = (r.u_up_t[...] * as_column(r.lam[4:5, :])).astype(bf16)
-    cols = block(i, UP_BLOCK)
     pre = (
-        mm(r.hid[...], columns(r.wup, cols))
-        + r.up_bias[:, cols].astype(f32)
+        mm(r.hid[...], flat(r.wup[t, x]))
+        + r.up_row[:, cols]
         + tmm(mixed_t, r.up_pt[:, cols])
     )
     phi = 0.5 * (1.0 + lax.erf(pre * np.float32(np.sqrt(0.5))))
@@ -387,15 +398,14 @@
 
 def down_reduce(r):
     r.u_down_t[...] = mm_t(r.down_qt[...], r.act[...])
-
-
-def down_project(r):
     mixed_t = (r.u_down_t[...] * as_column(r.lam[5:6, :])).astype(bf16)
-    r.branch[...] = (
-        mm_t(r.act[...], whole(r.wdown))
-        + r.down_bias[...].astype(f32)
-        + tmm(mixed_t, r.down_pt[...])
-    )
+    r.branch[...] = r.down_row[...] + tmm(mixed_t, r.down_pt[...])
+
+
+def down_third(t, r):
+    act = jnp.concatenate([r.act[:, third(t, x)] for x in range(2)], axis=1)
+    weight = jnp.concatenate([flat(r.wdown[t, x]) for x in range(2)], axis=1)
+    r.branch[...] += mm_t(act, weight)
 
 
 def norm_two(r):
@@ -425,22 +435,20 @@
     return jnp.transpose(jnp.broadcast_to(column, (column.shape[0], 128)))[0:1, :]
 
 
-BACK_BLOCK = 1024
-
-
 def down_back(r):
     gb = r.gb5[...]
     dp, du, dlam = back_factors(gb, r.down_pt[...], r.u_down_t[...], as_column(r.lam[5:6, :]))
     r.grad_narrow[R:, :] = dp
     r.grad_lam[5:6, 0:R] = as_row(jnp.sum(dlam, axis=1, keepdims=True))[:, 0:R]
 
-    def part(i):
-        cols = block(i, BACK_BLOCK)
-        grad = mm(gb, columns(r.wdown, cols)) + tmm(du, r.down_qt[:, cols])
-        r.grad_wide[R:, cols] = mm(du, r.act[:, cols])
-        r.gpre[:, cols] = (grad * r.slope[:, cols].astype(f32)).astype(bf16)
-
-    loop(FF // BACK_BLOCK, part)
+    def part(t):
+        for x in range(2):
+            cols = third(t, x)
+            grad = mm(gb, flat(r.wdown[t, x])) + tmm(du, r.down_qt[:, cols])
+            r.grad_wide[R:, cols] = mm(du, r.act[:, cols])
+            r.gpre[:, cols] = (grad * r.slope[:, cols].astype(f32)).astype(bf16)
+
+    loop(3, part)
 
 
 def up_back(r):
@@ -449,7 +457,7 @@
     r.grad_wide[:R, :] = dp
     r.grad_lam[4:5, 0:R] = as_row(jnp.sum(dlam, axis=1, keepdims=True))[:, 0:R]
     r.grad_narrow[:R, :] = mm(du, r.hid[...])
-    r.branch[...] = mm_t(gb, whole(r.wup)) + tmm(du, r.up_qt[...])
+    r.branch[...] = mm_t(gb, whole_wide(r.wup)) + tmm(du, r.up_qt[...])
     gain = r.norm_gain[0:1, :].astype(f32)
 
     def part(i):
@@ -567,7 +575,6 @@
 MESH = pl.DeviceIdType.MESH
 SLOTS = 6
 ALL = slice(None)
-WIDTH = dict(wqkv=384, wout=384, wup=1536, wdown=1536, embed=384)
 
 
 class Gather:
@@ -593,18 +600,17 @@
         pl.semaphore_wait(barrier, len(partners))
 
     def region(self, p, z, y, c, x):
-        name, lead, start, count, _ = self.parts[p]
+        name, lead, _ = self.parts[p]
         ref = getattr(self.r, name)
         ref = ref if lead is None else ref.at[lead]
-        width = WIDTH[name]
-        cols = ALL if x is None else pl.ds(pl.multiple_of(x * width, 128), width)
-        return ref.at[z, y, c, pl.ds(start, count), cols]
+        return ref.at[ALL if x is None else x, z, y, c]
 
     def shard(self, p):
-        name, lead, start, count, _ = self.parts[p]
+        name, lead, _ = self.parts[p]
         ref = getattr(self.r, name + "_shard")
-        ref = ref if lead is None else ref.at[lead]
-        return ref.at[pl.ds(start, count), :]
+        if lead is None:
+            return ref
+        return ref.at[lead] if name == "wqkv" else ref.at[:, pl.ds(lead * THIRD, THIRD)]
 
     def remote(self, source, target, p, slot, device):
         return pltpu.make_async_remote_copy(
@@ -626,7 +632,7 @@
         return self.region(p, z, y, c, None if "x" in done else self.x)
 
     def outgoing(self, p, k, own=None):
-        route = self.parts[p][4]
+        route = self.parts[p][2]
         region = self.held(p, route[:k], self.c)
         source = region if own is None else own
         if route[k] == "z":
@@ -636,7 +642,7 @@
         return [self.remote(source, region, p, k, device) for device in devices]
 
     def arriving(self, p, k, c):
-        route = self.parts[p][4]
+        route = self.parts[p][2]
         done = route[:k]
         z = ALL if "z" in done else self.z
         y = ALL if "y" in done else self.y
@@ -648,19 +654,19 @@
         return [self.region(p, z, y, c, 1 - self.x)]
 
     def amount(self, p, k):
-        route = self.parts[p][4]
+        route = self.parts[p][2]
         if route[k] != "z":
             return self.held(p, route[:k], self.c)
         y = ALL if "y" in route[:k] else self.y
         return self.region(p, pl.ds(0, 3), y, self.c, None if "x" in route[:k] else self.x)
 
     def sibling(self, p, k, c):
-        regions = [self.held(p, self.parts[p][4][:1], c)] if k == 0 else self.arriving(p, k, c)
+        regions = [self.held(p, self.parts[p][2][:1], c)] if k == 0 else self.arriving(p, k, c)
         device = self.device(c=1 - self.c)
         return [self.remote(ref, ref, p, 3 + k, device) for ref in regions]
 
     def sibling_amount(self, p, k):
-        ref = self.held(p, self.parts[p][4][:1], self.c) if k == 0 else self.amount(p, k)
+        ref = self.held(p, self.parts[p][2][:1], self.c) if k == 0 else self.amount(p, k)
         return self.remote(ref, ref, p, 3 + k, self.device(c=1 - self.c))
 
     def start(self, copies):
@@ -761,17 +767,19 @@
         self.swap_copy().wait_recv()
         comm = self.comm
         for x in range(2):
-            self.mine[x] = self.pack[x, comm.c] + self.swap[x]
+            for chip in range(8):
+                total = self.pack[x, comm.c, chip] + self.swap[x, chip]
+                self.mine[x, chip] = total.reshape(self.mine.shape[2:]).astype(bf16)
         for copy in self.chip_copies():
             copy.start()
         self.terms[comm.x * 8 + self.chip] = self.mine[comm.x, self.chip]
 
     def add(self):
         self.all_copies(1).wait_recv()
-        total = self.terms[0]
+        total = self.terms[0].astype(f32)
         for index in range(1, 16):
-            total = total + self.terms[index]
-        self.sums[self.chip * 2 + self.comm.c] = total
+            total = total + self.terms[index].astype(f32)
+        self.sums[self.chip * 2 + self.comm.c] = total.astype(bf16)
         for copy in self.sum_copies():
             copy.start()
 
@@ -789,23 +797,23 @@
     return {
         "pack_" + name: ((2, 2, 8) + tiles, f32),
         "swap_" + name: ((2, 8) + tiles, f32),
-        "mine_" + name: ((2, 8) + tiles, f32),
-        "terms_" + name: ((16,) + tiles, f32),
+        "mine_" + name: ((2, 8, count // 2, 16, 128), bf16),
+        "terms_" + name: ((16, count // 2, 16, 128), bf16),
     }
 
 
 PARTS = (
-    ("embed", None, 0, 32, "zxy"),
-    ("wqkv", 0, 0, 48, "zyx"),
-    ("wqkv", 1, 0, 48, "zxy"),
-    ("wqkv", 2, 0, 48, "zyx"),
-    ("wout", None, 0, 48, "zyx"),
-    ("wup", None, 0, 16, "zxy"),
-    ("wup", None, 16, 16, "xzy"),
-    ("wup", None, 32, 16, "zyx"),
-    ("wdown", None, 0, 16, "zyx"),
-    ("wdown", None, 16, 16, "xyz"),
-    ("wdown", None, 32, 16, "zxy"),
+    ("embed", None, "zxy"),
+    ("wqkv", 0, "zyx"),
+    ("wqkv", 1, "zxy"),
+    ("wqkv", 2, "zyx"),
+    ("wout", None, "zyx"),
+    ("wup", 0, "zxy"),
+    ("wup", 1, "xzy"),
+    ("wup", 2, "zyx"),
+    ("wdown", 0, "zyx"),
+    ("wdown", 1, "xyz"),
+    ("wdown", 2, "zxy"),
 )
 PLAN = (
     ("b", 0),
@@ -841,9 +849,9 @@
     (0, 7),
     (2, 2),
     ("s", "pos2"),
-    ("s", "pos3"),
     (2, 3),
     (0, 8),
+    ("s", "pos3"),
     (1, 4),
     ("s", "qkv0"),
     ("s", "qkv1"),
@@ -851,8 +859,8 @@
     ("s", "qkv3"),
     (1, 5),
     (0, 10),
+    ("s", "qkv4"),
     (1, 7),
-    ("s", "qkv4"),
     ("s", "attend0.0"),
     ("s", "attend0.1"),
     ("s", "attend1.0"),
@@ -860,30 +868,32 @@
     ("s", "attend1.1"),
     (2, 4),
     ("s", "attend2.0"),
+    ("s", "attend2.1"),
     (1, 6),
-    ("s", "attend2.1"),
     ("s", "attend3.0"),
     (1, 10),
     ("s", "attend3.1"),
+    ("s", "attend4.0"),
     (2, 5),
-    ("s", "attend4.0"),
     ("s", "attend4.1"),
     ("s", "attend5.0"),
     ("s", "attend5.1"),
     ("s", "out"),
     (2, 7),
+    ("s", "up0"),
     (2, 6),
-    ("s", "up0"),
     ("s", "up1"),
-    (2, 9),
     ("s", "up2"),
     ("s", "up3"),
-    (2, 8),
+    (2, 9),
     ("s", "up4"),
     ("s", "up5"),
+    (2, 8),
+    ("s", "down"),
     ("s", "down0"),
     (2, 10),
     ("s", "down1"),
+    ("s", "down2"),
 )
 
 
@@ -901,9 +911,11 @@
     qkv4=(arrange_heads, ()),
     attend=(attend, ()),
     out=(out_project, ("wout",)),
-    up=(up_project, ("wup",)),
-    down0=(down_reduce, ()),
-    down1=(down_project, ("wdown",)),
+    up=(up_project, ()),
+    down=(down_reduce, ()),
+    down0=(functools.partial(down_third, 0), (("wdown", 0),)),
+    down1=(functools.partial(down_third, 1), (("wdown", 1),)),
+    down2=(functools.partial(down_third, 2), (("wdown", 2),)),
 )
 BACKWARD = (
     norm_two,
@@ -917,47 +929,56 @@
     ready = set()
     waiting = []
     turns = {}
-    counts = dict(attend=H, up=FF // UP_BLOCK)
-
-    def moves(items):
-        for move in items:
-            comm.event(*move)
+    counts = dict(attend=H, up=6)
+
+    def act(items):
+        for kind, arg in items:
+            if kind == "r":
+                comm.ready(arg)
+            else:
+                comm.event(arg, kind)
 
     def before(*turn):
         for place, items in turns.items():
             if items and place[1:] == turn[1:]:
-                pl.when(turn[0] == place[0])(functools.partial(moves, items))
+                pl.when(turn[0] == place[0])(functools.partial(act, items))
+
+    def need(parts):
+        for p, part in enumerate(comm.parts):
+            if p not in ready and (part[0] in parts or part[:2] in parts):
+                ready.add(p)
+                waiting.append(("r", p))
 
     for kind, arg in plan:
         if kind == "b":
             comm.begin(arg)
             continue
         if kind != "s":
-            waiting.append((arg, kind))
+            waiting.append((kind, arg))
             continue
         name = arg.rstrip("0123456789.")
-        looped = name in counts
-        step, needs = STEPS[name if looped else arg]
-        if not looped or not turns:
-            moves(waiting)
-            waiting = []
-            for p, part in enumerate(comm.parts):
-                if p not in ready and (part[0] in needs or part[:2] in needs):
-                    comm.ready(p)
-                    ready.add(p)
-        if not looped:
+        if name not in counts:
+            step, needs = STEPS[arg]
+            need(needs)
+            act(waiting)
+            waiting.clear()
             step(r)
             continue
-        turns[tuple(int(c) for c in arg[len(name) :].split("."))] = waiting
-        waiting = []
+        turn = tuple(int(c) for c in arg[len(name) :].split("."))
+        if name == "up":
+            need((("wup", turn[0] // 2),))
+        turns[turn] = list(waiting)
+        waiting.clear()
         if len(turns) == counts[name]:
-            step(r, before)
+            STEPS[name][0](r, before)
             turns = {}
-    moves(waiting)
+    act(waiting)
 
 
 EARLY, LATE = 4, 2
-SUMS = dict(sums_early=((16, EARLY, 8, 128), f32), sums_late=((16, LATE, 8, 128), f32))
+SUMS = dict(
+    sums_early=((16, EARLY // 2, 16, 128), bf16), sums_late=((16, LATE // 2, 16, 128), bf16)
+)
 FUSED_SCRATCH = {
     **SCRATCH,
     **GATHERED,
@@ -998,7 +1019,7 @@
 
     def before(p):
         pl.when(p == 1)(early.spread)
-        pl.when(p == 3)(early.add)
+        pl.when(p == 4)(early.add)
 
     attend_back(r, before)
     qkv_factors(r)
@@ -1023,16 +1044,18 @@
     grad_out[...] = grad_in[...]
     wide, narrow, fourth, attn = parts
     for sums, refs in ((early, (wide, narrow, fourth)), (late, (attn,))):
-        count = sums.shape[1]
+        count = 2 * sums.shape[1]
         tile = 0
         for ref in refs:
             for row in range(ref.shape[0] // 8):
                 for col in range(ref.shape[1] // 128):
                     core, chip, slot = tile // (8 * count), tile // count % 8, tile % count
-                    ref[8 * row : 8 * row + 8, 128 * col : 128 * col + 128] = sums[chip * 2 + core, slot]
+                    pair = sums[chip * 2 + core, slot // 2].astype(f32)
+                    half = slice(8 * (slot % 2), 8 * (slot % 2) + 8)
+                    ref[8 * row : 8 * row + 8, 128 * col : 128 * col + 128] = pair[half, :]
                     tile += 1
     core, chip, slot = tile // (8 * count), tile // count % 8, tile % count
-    lam = sums[chip * 2 + core, slot]
+    lam = sums[chip * 2 + core, slot // 2].astype(f32)[8 * (slot % 2) : 8 * (slot % 2) + 8, :]
     for n in range(4):
         glam[n : n + 1, :] = lam[0:1, R * n : R * (n + 1)]
     glam[4:6, :] = lam[4:6, 0:R]
@@ -1075,6 +1098,15 @@
     )(layer_out, grad_tokens, early, late)
 
 
+def arrange_weight(weight, shape):
+    *lead, rows, cols = weight.shape
+    if shape[-1] == THIRD:
+        split = weight.reshape(rows, 2, 3, THIRD)
+        return jnp.transpose(split, (2, 1, 0, 3)).reshape(shape)
+    split = weight.reshape(*lead, rows, 2, cols // 2)
+    return jnp.moveaxis(split, -2, len(lead)).reshape(shape)
+
+
 def layer_call(args, weights, fused):
     vmem = pl.BlockSpec(memory_space=pltpu.VMEM)
     hbm = pl.BlockSpec(memory_space=pl.ANY)
@@ -1093,7 +1125,7 @@
     else:
         outputs = OUTPUTS + list(GRADS)
         scratch = [pltpu.VMEM(*spec) for spec in SCRATCH.values()] + [load_sem]
-        weights = [w.reshape(GATHERED[name][0]) for name, w in zip(GATHERED, weights)]
+        weights = [arrange_weight(w, GATHERED[name][0]) for name, w in zip(GATHERED, weights)]
         extra = {}
     return pl.pallas_call(
         functools.partial(layer_kernel, fused),
@@ -1161,8 +1193,8 @@
         segments,
         jnp.asarray(bucket_rows()),
         attn_bias,
-        up_bias[None],
-        down_bias[None],
+        up_bias,
+        down_bias,
         norm_gain,
         norm_bias,
         jnp.transpose(attn_p, (2, 1, 0)),

time: 144 us -> 137 us (0.951)
  Pallas kernels: 141 us -> 136 us
  local copies, waits for them, and re-layouts: 1.86 us -> 0 us
    pallas_call x1, Pallas kernels: 139 us -> 133 us  [layer_call(): pl.pallas_call(functools.partial(layer_kernel, fused), out_shape=[jax.Sha...]
where the time goes in v1:
time: 137 us
  Pallas kernels  136 us (99%)
    pallas_call x1, Pallas kernels, layer_call(): pl.pallas_call(functools.partial(layer_kernel, fused), out_shape=[jax.Sha...  133 us

profile of v1, /device:TPU:0, one launch (start us, length us, event | category | flops | bytes accessed | tf_op | source)
XLA Modules:
  0.0 136.7 jit_solution(15683401823992887302)
XLA Ops:
  0.7 133.3 %shard_map.268 = (bf16[512,768]{1,0:T(8,128)(2,1)}, bf16[512,768]{1,0:T(8,128)(2,1)}, bf16[16,2,16,128]{3,2,1,0:T(8,128)(2,1)}, bf16[16,1,16,128]{3,2,1,0:T(8,128)(2,1)}) custom-call(bf16[512,768]{1,0:T(8,128)(2,1)} %refs_0_.1, bf16[512,768]{1,0:T(8,128)(2,1)} %refs_1_.1, s32[1,512]{1,0:T(1,128)} %refs_2_.1, s32[2,512]{1,0:T(2,128)} %constant.2.clone.refs_3_, ...), custom_call_target="tpu_custom_call" | custom-call | tf_op jit(solution)/shard_map/pallas_call | solution.py:1130
  134.0 2.7 %shard_map.269 = (bf16[512,768]{1,0:T(8,128)(2,1)}, bf16[512,768]{1,0:T(8,128)(2,1)}, f32[12,4,384]{2,1,0:T(4,128)}, f32[12,4,384]{2,1,0:T(4,128)}, f32[12,1536]...) custom-call(bf16[512,768]{1,0:T(8,128)(2,1)} %get-tuple-element.22.layer_in, ...), custom_call_target="tpu_custom_call" | custom-call | tf_op jit(solution)/shard_map/pallas_call | solution.py:1087

commit v2 on v1

--- a/solution.py
+++ b/solution.py
@@ -513,10 +513,12 @@
                 turn_t = pltpu.roll(gs_t, 0, 1, stride=1, stride_axis=0)
                 fro = jnp.concatenate([jnp.where(low, turn_t, zero), jnp.where(low, zero, turn_t)], axis=1)
                 queries, keys = r.qt[feats[a], rows], r.k_rev_t[feats[a], rows]
-                gq = mm(keys, gs_t) + mm_t(r.pk_far_t[feats[a], :], to)
-                gk = mm(queries, gs) + mm_t(r.pq_far_t[feats[a], :], fro)
+                query_part = mm(queries, jnp.concatenate([gs, to], axis=1))
+                key_part = mm(keys, jnp.concatenate([gs_t, fro], axis=1))
+                gk = query_part[:, :HALF] + mm_t(r.pq_far_t[feats[a], :], fro)
                 gv = mm(r.g_t[feats[a], rows], r.probs[2 * p + a, rows, :])
-                gpk_b, gpq_b = mm(queries, to), mm(keys, fro)
+                gq = key_part[:, :HALF] + mm_t(r.pk_far_t[feats[a], :], to)
+                gpk_b, gpq_b = query_part[:, HALF:], key_part[:, HALF:]
                 gpk = gpk_b if gpk is None else gpk + gpk_b
                 gpq = gpq_b if gpq is None else gpq + gpq_b
                 stores.append((r.gq_t, feats[a], rows, gq * SCALE))

time: 137 us -> 135 us (0.985)
  Pallas kernels: 136 us -> 134 us
    pallas_call x1, Pallas kernels: 133 us -> 132 us  [layer_call(): pl.pallas_call(functools.partial(layer_kernel, fused), out_shape=[jax.Sha...]
where the time goes in v2:
time: 135 us
  Pallas kernels  134 us (99%)
    pallas_call x1, Pallas kernels, layer_call(): pl.pallas_call(functools.partial(layer_kernel, fused), out_shape=[jax.Sha...  132 us
    pallas_call x1, Pallas kernels, unpack_call(): pl.pallas_call(unpack_kernel, out_shape=[jax.ShapeDtypeStruct(*shape) for...  2.71 us

profile of v2, /device:TPU:0, one launch (start us, length us, event | category | flops | bytes accessed | tf_op | source)
XLA Modules:
  0.0 134.9 jit_solution(4006769696112785702)
XLA Ops:
  0.7 131.5 %shard_map.268 = (bf16[512,768]{1,0:T(8,128)(2,1)}, bf16[512,768]{1,0:T(8,128)(2,1)}, bf16[16,2,16,128]{3,2,1,0:T(8,128)(2,1)}, bf16[16,1,16,128]{3,2,1,0:T(8,128)(2,1)}) custom-call(bf16[512,768]{1,0:T(8,128)(2,1)} %refs_0_.1, bf16[512,768]{1,0:T(8,128)(2,1)} %refs_1_.1, s32[1,512]{1,0:T(1,128)} %refs_2_.1, s32[2,512]{1,0:T(2,128)} %constant.2.clone.refs_3_, ...), custom_call_target="tpu_custom_call" | custom-call | tf_op jit(solution)/shard_map/pallas_call | solution.py:1132
  132.2 2.7 %shard_map.269 = (bf16[512,768]{1,0:T(8,128)(2,1)}, bf16[512,768]{1,0:T(8,128)(2,1)}, f32[12,4,384]{2,1,0:T(4,128)}, f32[12,4,384]{2,1,0:T(4,128)}, f32[12,1536]...) custom-call(bf16[512,768]{1,0:T(8,128)(2,1)} %get-tuple-element.22.layer_in, ...), custom_call_target="tpu_custom_call" | custom-call | tf_op jit(solution)/shard_map/pallas_call | solution.py:1089

commit v3 on v2

--- a/solution.py
+++ b/solution.py
@@ -412,7 +412,7 @@
     gain, bias = r.norm_gain[1:2, :].astype(f32), r.norm_bias[1:2, :].astype(f32)
 
     def part(i):
-        rows = block(i, 128)
+        rows = block(i, 256)
         total = r.hidden[rows, :] + r.branch[rows, :]
         centre = total - mean_row(total)
         rs = lax.rsqrt(mean_row(centre * centre) + EPS)
@@ -423,7 +423,7 @@
         r.gsum2[rows, :] = grad
         r.gb5[rows, :] = grad.astype(bf16)
 
-    loop(L // 128, part)
+    loop(L // 256, part)
 
 
 def back_factors(gb, p_t, u_t, lam):
@@ -461,14 +461,14 @@
     gain = r.norm_gain[0:1, :].astype(f32)
 
     def part(i):
-        rows = block(i, 128)
+        rows = block(i, 256)
         e = (r.gsum2[rows, :] + r.branch[rows, :]) * gain
         xhat = r.xhat1[rows, :]
         grad = r.rs1[rows, :] * (e - mean_row(e) - xhat * mean_row(e * xhat))
         r.gsum1[rows, :] = grad
         r.gb3[rows, :] = grad.astype(bf16)
 
-    loop(L // 128, part)
+    loop(L // 256, part)
 
 
 def out_back(r):
@@ -638,7 +638,10 @@
         region = self.held(p, route[:k], self.c)
         source = region if own is None else own
         if route[k] == "z":
-            devices = [self.device(z=(self.z + j) % 4) for j in (1, 2, 3)]
+            far = self.z // 2
+            near = self.z * (1 - 2 * far) + 3 * far
+            targets = [(3 * far + (1 - 2 * far) * place) for place in (3, 2, 1 - near)]
+            devices = [self.device(z=target) for target in targets]
         else:
             devices = [self.device(y=1 - self.y) if route[k] == "y" else self.device(x=1 - self.x)]
         return [self.remote(source, region, p, k, device) for device in devices]

time: 135 us -> 135 us (level)
  no operation moved by 1% of the time
where the time goes in v3:
time: 135 us
  Pallas kernels  134 us (99%)
    pallas_call x1, Pallas kernels, layer_call(): pl.pallas_call(functools.partial(layer_kernel, fused), out_shape=[jax.Sha...  132 us
    pallas_call x1, Pallas kernels, unpack_call(): pl.pallas_call(unpack_kernel, out_shape=[jax.ShapeDtypeStruct(*shape) for...  2.71 us

profile of v3, /device:TPU:0, one launch (start us, length us, event | category | flops | bytes accessed | tf_op | source)
XLA Modules:
  0.0 135.1 jit_solution(14352410396295617560)
XLA Ops:
  0.7 131.7 %shard_map.268 = (bf16[512,768]{1,0:T(8,128)(2,1)}, bf16[512,768]{1,0:T(8,128)(2,1)}, bf16[16,2,16,128]{3,2,1,0:T(8,128)(2,1)}, bf16[16,1,16,128]{3,2,1,0:T(8,128)(2,1)}) custom-call(bf16[512,768]{1,0:T(8,128)(2,1)} %refs_0_.1, bf16[512,768]{1,0:T(8,128)(2,1)} %refs_1_.1, s32[1,512]{1,0:T(1,128)} %refs_2_.1, s32[2,512]{1,0:T(2,128)} %constant.2.clone.refs_3_, ...), custom_call_target="tpu_custom_call" | custom-call | tf_op jit(solution)/shard_map/pallas_call | solution.py:1135
  132.4 2.7 %shard_map.269 = (bf16[512,768]{1,0:T(8,128)(2,1)}, bf16[512,768]{1,0:T(8,128)(2,1)}, f32[12,4,384]{2,1,0:T(4,128)}, f32[12,4,384]{2,1,0:T(4,128)}, f32[12,1536]...) custom-call(bf16[512,768]{1,0:T(8,128)(2,1)} %get-tuple-element.22.layer_in, ...), custom_call_target="tpu_custom_call" | custom-call | tf_op jit(solution)/shard_map/pallas_call | solution.py:1092
